TPU v7x, 32 devices: a whole 2x2x4 slice. The times are simulated.
32 devices in a mesh: group: 2 (over y), expert: 4 (over z), head: 4 (over x, core).
Axes of the slice: x: 2, y: 2, z: 4, core: 2. Of those that a mesh axis runs over, the one named last changes fastest.
Arguments:
- q_latent: bfloat16 [512, 32768], P(('group', 'expert'), 'head'), parts along dimension 0, may hold values from -100 to 100
- q_rope: bfloat16 [512, 4096], P(('group', 'expert'), 'head'), parts along dimension 0, may hold values from -100 to 100
- prefix_latent: bfloat16 [128, 512], P(('group', 'expert')), parts along dimension 0, may hold values from -6 to 6
- prefix_rope: bfloat16 [128, 64], P(('group', 'expert')), parts along dimension 0, may hold values from -6 to 6
- span_latent: bfloat16 [512, 512], P(('group', 'expert')), parts along dimension 0, may hold values from -6 to 6
- span_rope: bfloat16 [512, 64], P(('group', 'expert')), parts along dimension 0, may hold values from -6 to 6
- prefix_len: int32 [2], P('group'), parts along dimension 0, may hold values from 16 to 64
- moe_input: bfloat16 [512, 7168], P(('group', 'expert'), 'head'), parts along dimension 0, may hold values from -6 to 6
- routes: int32 [512, 2], P(('group', 'expert')), parts along dimension 0, may hold values from 0 to 3, all different within a row; in each aligned block of 64 rows (0 to 63, 64 to 127, ...) at most 36 rows name the same one
- owners: int32 [8], P('group'), parts along dimension 0, may hold values from 0 to 3, each once
- gate_weight: bfloat16 [4, 7168, 1024], P('expert', None, 'head'), may hold values from -0.0625 to 0.0625
- up_weight: bfloat16 [4, 7168, 1024], P('expert', None, 'head'), may hold values from -0.0625 to 0.0625
Outputs:
- attended: bfloat16 [512, 32768], P(('group', 'expert'), 'head'), parts along dimension 0
- expert_hidden: bfloat16 [8, 144, 1024], P(('group', 'expert'), None, 'head'), parts along dimension 0
- migrated_latent: bfloat16 [640, 512], P(('group', 'expert')), parts along dimension 0
- migrated_rope: bfloat16 [640, 64], P(('group', 'expert')), parts along dimension 0
There are 2 independent parts, one for each index of `group`. A program takes and returns all parts, laid end to end along the dimension named above; an argument that names none is the same for every part. Nothing has to cross between parts.
Inputs may be any that keep to these rules, and one draw needn't show every extreme that they name: `routes`: among the 64 rows of one device no expert is named by more than 36 rows, a bound that some block reaches. `owners`: A permutation of 0 to 3.
All inputs are finite; a program needn't handle non-finite values.
Results may differ from a plain program's by a relative error of at most 0.0049.
Values may be sent and summed in bfloat16 or wider, within the bound.
A program may use at most 128 MiB of HBM per device.

v0:
```python
import jax
import jax.numpy as jnp
from jax import lax
from jax.sharding import PartitionSpec as P

LATENT = 512
ROPE = 64


softmax_scale = 192.0 ** (-0.5)


def body(
    q_latent,
    q_rope,
    prefix_latent,
    prefix_rope,
    span_latent,
    span_rope,
    prefix_len,
    moe_input,
    routes,
    owners,
    gate_weight,
    up_weight,
):
    own_index = lax.axis_index("expert")
    dev_count = lax.axis_size("expert")
    tok_rows = span_latent.shape[0]
    pre_rows = prefix_latent.shape[0]
    block_rows = pre_rows + tok_rows
    heads_here = q_rope.shape[1] // ROPE
    limit = prefix_len[0]
    prefix_pos = own_index * pre_rows + jnp.arange(pre_rows, dtype=jnp.int32)
    prefix_kept = prefix_pos < limit
    cache_latent = jnp.concatenate(
        [
            jnp.where(prefix_kept[:, None], prefix_latent, jnp.zeros_like(prefix_latent)),
            span_latent,
        ],
        axis=0,
    )
    cache_rope = jnp.concatenate(
        [jnp.where(prefix_kept[:, None], prefix_rope, jnp.zeros_like(prefix_rope)), span_rope],
        axis=0,
    )
    query_lat = q_latent.reshape(tok_rows * heads_here, LATENT)
    query_rot = q_rope.reshape(tok_rows * heads_here, ROPE)
    query_count = tok_rows * heads_here
    query_pos = jnp.repeat(own_index * tok_rows + jnp.arange(tok_rows, dtype=jnp.int32), heads_here)
    contract_dims = (((1,), (1,)), ((), ()))
    peak_old = jnp.full((query_count,), -1e30, jnp.float32)
    lat_piece = lax.all_gather(cache_latent, "expert", axis=0, tiled=True)
    rot_piece = lax.all_gather(cache_rope, "expert", axis=0, tiled=True)
    count_rows = lat_piece.shape[0]
    position = jnp.arange(count_rows, dtype=jnp.int32)
    source = position // block_rows
    within = position % block_rows
    in_prefix = within < pre_rows
    prefix_ok = source * pre_rows + within < limit
    span_pos = source * tok_rows + within - pre_rows
    allowed = jnp.where(
        in_prefix[None, :], prefix_ok[None, :], span_pos[None, :] <= query_pos[:, None]
    )
    scores = lax.dot_general(
        query_lat, lat_piece, contract_dims, preferred_element_type=jnp.float32
    )
    scores = (
        scores
        + lax.dot_general(query_rot, rot_piece, contract_dims, preferred_element_type=jnp.float32)
    ) * softmax_scale
    masked = jnp.where(allowed, scores, -1e30)
    peak_new = jnp.maximum(peak_old, jnp.max(masked, axis=1))
    weights = jnp.where(allowed, jnp.exp(masked - peak_new[:, None]), 0.0)
    total_new = jnp.sum(weights, axis=1)
    accum_new = jnp.dot(weights.astype(jnp.bfloat16), lat_piece, preferred_element_type=jnp.float32)
    target = owners[own_index]
    chosen = (jnp.arange(dev_count, dtype=jnp.int32) == target)[:, None, None]
    outgoing_lat = jnp.where(
        chosen, cache_latent[None], jnp.zeros((dev_count, block_rows, LATENT), jnp.bfloat16)
    )
    outgoing_rot = jnp.where(
        chosen, cache_rope[None], jnp.zeros((dev_count, block_rows, ROPE), jnp.bfloat16)
    )
    incoming_lat, incoming_rot = (
        lax.all_to_all(outgoing_lat, "expert", split_axis=0, concat_axis=0, tiled=True),
        lax.all_to_all(outgoing_rot, "expert", split_axis=0, concat_axis=0, tiled=True),
    )
    migrated_latent = jnp.sum(incoming_lat.astype(jnp.float32), axis=0).astype(jnp.bfloat16)
    migrated_rope = jnp.sum(incoming_rot.astype(jnp.float32), axis=0).astype(jnp.bfloat16)
    attended = (
        (accum_new / total_new[:, None]).astype(jnp.bfloat16).reshape(tok_rows, heads_here * LATENT)
    )
    top_count = routes.shape[1]
    capacity = min(tok_rows, max(2, 9 * tok_rows * top_count // (8 * dev_count)))
    expert_ids = jnp.arange(dev_count, dtype=jnp.int32)
    routed = jnp.any(routes[:, :, None] == expert_ids[None, None, :], axis=1).astype(jnp.float32)
    token_ids = jnp.arange(tok_rows, dtype=jnp.int32)
    lower_ones = (token_ids[:, None] >= token_ids[None, :]).astype(jnp.float32)
    slot_rank = jnp.dot(lower_ones, routed) - 1.0
    slot_ids = jnp.arange(capacity, dtype=jnp.int32).astype(jnp.float32)
    dispatch = (
        (routed.T[:, None, :] > 0.5) & (slot_rank.T[:, None, :] == slot_ids[None, :, None])
    ).astype(jnp.bfloat16)
    w_gate = gate_weight[0]
    w_up = up_weight[0]
    features = lax.all_gather(moe_input, "head", axis=1, tiled=True)
    outgoing = jnp.einsum(
        "ect,td->ecd", dispatch, features, preferred_element_type=jnp.float32
    ).astype(jnp.bfloat16)
    incoming = lax.all_to_all(outgoing, "expert", split_axis=0, concat_axis=0, tiled=True)
    expert_rows = incoming.reshape(dev_count * capacity, incoming.shape[2])
    gated = jnp.dot(expert_rows, w_gate, preferred_element_type=jnp.float32)
    upward = jnp.dot(expert_rows, w_up, preferred_element_type=jnp.float32)
    expert_hidden = (jax.nn.silu(gated) * upward).astype(jnp.bfloat16)[None]
    return (attended, expert_hidden, migrated_latent, migrated_rope)


def solution(mesh):
    in_specs = (
        P(("group", "expert"), "head"),
        P(("group", "expert"), "head"),
        P(("group", "expert"), None),
        P(("group", "expert"), None),
        P(("group", "expert"), None),
        P(("group", "expert"), None),
        P("group"),
        P(("group", "expert"), "head"),
        P(("group", "expert"), None),
        P("group"),
        P("expert", None, "head"),
        P("expert", None, "head"),
    )
    out_specs = (
        P(("group", "expert"), "head"),
        P(("group", "expert"), None, "head"),
        P(("group", "expert"), None),
        P(("group", "expert"), None),
    )
    return jax.shard_map(body, mesh=mesh, in_specs=in_specs, out_specs=out_specs, check_vma=False)
```

profile of v0, /device:TPU:0, one launch (start us, length us, event | category | flops | bytes accessed | tf_op | source)
XLA Modules:
  0.0 129.1 jit_solution(6551876463626626039)
XLA Ops:
  1.3 1.2 dynamic_slice.3
  2.5 0.6 iota_compare_fusion.3
  3.2 0.8 copy.26
  4.0 0.8 copy.25
  4.9 0.7 broadcast_select_fusion.1
  5.6 6.3 %all-to-all-start.2 = ((bf16[4,80,64]{1,2,0:T(8,128)(2,1)}), bf16[4,80,64]{1,2,0:T(8,128)(2,1)S(1)}, u32[]{:S(2)}, u32[]{:S(2)}) async-start(bf16[4,80,64]{1,2,0:T(8,128)(2,1)} %broadcast_select_fusion.1), calls=%async_computation.2 | async-start | bytes 131072 | tf_op jit(solution)/shard_map/all_to_all | solution.py:87
  11.9 0.7 fusion.31
  12.7 0.8 broadcast_select_fusion.2
  13.5 0.8 pad_maximum_fusion
  14.4 0.8 broadcast_select_fusion
  15.2 9.5 %all_gather.11 = bf16[64,7168]{1,0:T(8,128)(2,1)S(1)} all-gather(bf16[64,1792]{1,0:T(8,128)(2,1)} %param.19), channel_id=1, replica_groups=mesh['group'=2,'expert'=4,'head'=4] {'head'}, dimensions={1}, use_global_device_ids=true | all-gather | bytes 1146880 | tf_op jit(solution)/shard_map/all_gather | solution.py:107
  24.7 5.1 %all-to-all-start.1 = ((bf16[4,80,512]{2,1,0:T(8,128)(2,1)}), bf16[4,80,512]{2,1,0:T(8,128)(2,1)S(1)}, u32[]{:S(2)}, u32[]{:S(2)}) async-start(bf16[4,80,512]{2,1,0:T(8,128)(2,1)} %broadcast_select_fusion), calls=%async_computation.1 | async-start | bytes 655360 | tf_op jit(solution)/shard_map/all_to_all | solution.py:86
  29.8 2.2 %convolution_convert_fusion = bf16[4,36,7168]{2,1,0:T(8,128)(2,1)} fusion(bf16[64,7168]{1,0:T(8,128)(2,1)S(1)} %all_gather.11, f32[4,64]{1,0:T(4,128)S(1)} %convolution_add_fusion.1, f32[36]{0:T(128)S(1)} %iota_convert_fusion, pred[4,64]{1,0:T(4,128)(4,1)S(1)} %fusion.38), kind=kOutput, calls=%fused_computation | convolution fusion | flops 133171200 | bytes 2983312 | tf_op jit(solution)/shard_map/ect,td->ecd/dot_general | solution.py:108
  32.0 8.6 %all-to-all-done.1 = bf16[4,80,512]{2,1,0:T(8,128)(2,1)S(1)} async-done(((bf16[4,80,512]{2,1,0:T(8,128)(2,1)}), bf16[4,80,512]{2,1,0:T(8,128)(2,1)S(1)}, u32[]{:S(2)}, u32[]{:S(2)}) %all-to-all-start.1) | async-done | bytes 327712 | tf_op jit(solution)/shard_map/all_to_all | solution.py:86
  40.6 4.6 %all-to-all-start = ((bf16[4,36,7168]{2,1,0:T(8,128)(2,1)}), bf16[4,36,7168]{2,1,0:T(8,128)(2,1)}, u32[]{:S(2)}, u32[]{:S(2)}) async-start(bf16[4,36,7168]{2,1,0:T(8,128)(2,1)} %convolution_convert_fusion), calls=%async_computation | async-start | bytes 4587520 | tf_op jit(solution)/shard_map/all_to_all | solution.py:111
  45.5 56.4 %all-gather = bf16[4,80,64]{1,2,0:T(8,128)(2,1)S(1)} all-gather(bf16[1,80,64]{1,2,0:T(8,128)(2,1)S(1)} %fusion.50), channel_id=1, replica_groups=mesh['group'=2,'expert'=4,'head'=4] {'expert'}, dimensions={0}, use_global_device_ids=true | all-gather | bytes 51200 | tf_op jit(solution)/shard_map/all_gather | solution.py:54
  102.8 14.7 %all_gather.9 = bf16[320,512]{1,0:T(8,128)(2,1)S(1)} all-gather(bf16[80,512]{1,0:T(8,128)(2,1)S(1)} %pad_maximum_fusion), channel_id=1, replica_groups=mesh['group'=2,'expert'=4,'head'=4] {'expert'}, dimensions={0}, use_global_device_ids=true | all-gather | bytes 409600 | tf_op jit(solution)/shard_map/all_gather | solution.py:53
  119.1 1.0 divide_convert_fusion
  120.1 1.3 %reshape.76 = bf16[64,8192]{1,0:T(8,128)(2,1)} reshape(bf16[1024,512]{1,0:T(8,128)(2,1)S(1)} %divide_convert_fusion) | data formatting | bytes 2097152 | tf_op jit(solution)/shard_map/reshape | solution.py:92
  121.4 0.6 reduce_sum.35
  122.0 0.7 reduce_sum.34
  122.7 1.9 %reshape.77 = bf16[144,7168]{1,0:T(8,128)(2,1)S(1)} reshape(bf16[4,36,7168]{2,1,0:T(8,128)(2,1)} %all-to-all-done) | data formatting | bytes 4128768 | tf_op jit(solution)/shard_map/reshape | solution.py:112
  124.6 2.9 %fusion.2 = f32[144,256]{1,0:T(8,128)S(1)} fusion(bf16[144,7168]{1,0:T(8,128)(2,1)S(1)} %reshape.77, bf16[1,7168,256]{2,1,0:T(8,128)(2,1)} %param.22), kind=kOutput, calls=%fused_computation.3 | convolution fusion | flops 528482304 | bytes 5881856 | tf_op jit(solution)/shard_map/dot_general | solution.py:113
  127.7 1.4 %fusion.13 = bf16[1,144,256]{2,1,0:T(8,128)(2,1)} fusion(bf16[144,7168]{1,0:T(8,128)(2,1)S(1)} %reshape.77, bf16[1,7168,256]{2,1,0:T(8,128)(2,1)S(1)} %copy-done, f32[144,256]{1,0:T(8,128)S(1)} %fusion.2), kind=kOutput, calls=%fused_computation.14 | convolution fusion | flops 528703488 | bytes 5955584 | tf_op jit(solution)/shard_map/dot_general | solution.py:114
  (28 shorter events, 3.1 us)
Async XLA Ops:
  5.6 19.1 %all-to-all-start.2 = ((bf16[4,80,64]{1,2,0:T(8,128)(2,1)}), bf16[4,80,64]{1,2,0:T(8,128)(2,1)S(1)}, u32[]{:S(2)}, u32[]{:S(2)}) async-start(bf16[4,80,64]{1,2,0:T(8,128)(2,1)} %broadcast_select_fusion.1), calls=%async_computation.2 | async-start | bytes 131072 | tf_op jit(solution)/shard_map/all_to_all | solution.py:87
  24.7 15.9 %all-to-all-start.1 = ((bf16[4,80,512]{2,1,0:T(8,128)(2,1)}), bf16[4,80,512]{2,1,0:T(8,128)(2,1)S(1)}, u32[]{:S(2)}, u32[]{:S(2)}) async-start(bf16[4,80,512]{2,1,0:T(8,128)(2,1)} %broadcast_select_fusion), calls=%async_computation.1 | async-start | bytes 655360 | tf_op jit(solution)/shard_map/all_to_all | solution.py:86
  32.0 70.1 %copy-start.2 = (bf16[64,1024]{1,0:T(8,128)(2,1)S(1)}, bf16[64,1024]{1,0:T(8,128)(2,1)}, u32[]{:S(2)}) copy-start(bf16[64,1024]{1,0:T(8,128)(2,1)} %param.13) | copy-start | bytes 393220
  40.6 61.6 %copy-start.1 = (bf16[64,8192]{1,0:T(8,128)(2,1)S(1)}, bf16[64,8192]{1,0:T(8,128)(2,1)}, u32[]{:S(2)}) copy-start(bf16[64,8192]{1,0:T(8,128)(2,1)} %param.12) | copy-start | bytes 3145732
  40.6 82.1 %all-to-all-start = ((bf16[4,36,7168]{2,1,0:T(8,128)(2,1)}), bf16[4,36,7168]{2,1,0:T(8,128)(2,1)}, u32[]{:S(2)}, u32[]{:S(2)}) async-start(bf16[4,36,7168]{2,1,0:T(8,128)(2,1)} %convolution_convert_fusion), calls=%async_computation | async-start | bytes 4587520 | tf_op jit(solution)/shard_map/all_to_all | solution.py:111
  124.5 3.1 %copy-start = (bf16[1,7168,256]{2,1,0:T(8,128)(2,1)S(1)}, bf16[1,7168,256]{2,1,0:T(8,128)(2,1)}, u32[]{:S(2)}) copy-start(bf16[1,7168,256]{2,1,0:T(8,128)(2,1)} %param.23) | copy-start | bytes 11010052
where the time goes:
time: 130 us; the launch traced here: 129 us
  blocking collectives  80.6 us (62%)
  starting transfers between devices  16 us (12%)
  waiting for transfers between devices  8.63 us (7%)
  matrix products  8.62 us (7%)
  local copies, waits for them, and re-layouts  7.26 us (6%)
  other arithmetic  6.48 us (5%)
  between operations  1.44 us (1%)
    all_gather x1, blocking collectives, body(): rot_piece = lax.all_gather(cache_rope, 'expert', axis=0, tiled=True)  56.4 us
    all_gather x1, blocking collectives, body(): lat_piece = lax.all_gather(cache_latent, 'expert', axis=0, tiled=True)  14.7 us
    all_gather x1, blocking collectives, body(): features = lax.all_gather(moe_input, 'head', axis=1, tiled=True)  9.51 us
    all_to_all x1, waiting for transfers between devices, body(): lax.all_to_all(outgoing_lat, 'expert', split_axis=0, concat_axis=0, tiled...  8.63 us
    all_to_all x1, starting transfers between devices, body(): lax.all_to_all(outgoing_rot, 'expert', split_axis=0, concat_axis=0, tiled...  6.32 us
    all_to_all x1, starting transfers between devices, body(): lax.all_to_all(outgoing_lat, 'expert', split_axis=0, concat_axis=0, tiled...  5.09 us
    all_to_all x1, starting transfers between devices, body(): lax.all_to_all(outgoing, 'expert', split_axis=0, concat_axis=0, tiled=True)  4.61 us
    dot_general x1, matrix products, body(): gated = jnp.dot(expert_rows, w_gate, preferred_element_type=jnp.float32)  2.89 us
  transfers between devices with their start and end apart: 3, of which 1 were waited for; matrix products, arithmetic and copies ran while one was open for 9% of the time, Pallas kernels for 0%

commit v1 on v0

v1 whole, which is shorter than its diff:
```python
import functools

import jax
import jax.numpy as jnp
from jax import lax
from jax.experimental import pallas as pl
from jax.experimental.pallas import tpu as pltpu
from jax.sharding import PartitionSpec as P

SOFTMAX_SCALE = 192.0 ** (-0.5)
MESH = pl.DeviceIdType.MESH
NT = (((1,), (1,)), ((), ()))


def each(count, step):
    if count <= 4:
        for i in range(count):
            step(i)
    else:
        def one(i, carry):
            step(i)
            return carry
        lax.fori_loop(0, count, one, 0)


def each_from(first, count, step):
    each(count - first, lambda i: step(i + first))


class Plan:
    def __init__(self, n, heads_axis, tok, pre, lat, rope, heads, width, top, hidden):
        self.n, self.nh, self.nx = n, heads_axis, heads_axis // 2
        self.tok, self.pre, self.lat, self.rope, self.heads = tok, pre, lat, rope, heads
        self.block = tok + pre
        self.keys = n * self.block
        self.kw = lat + 2 * rope
        self.width, self.top, self.hidden = width, top, hidden
        self.cap = min(tok, max(2, 9 * tok * top // (8 * n)))
        self.cw = 256 if width % 256 == 0 else 128
        self.chunks = width // self.cw
        self.main = self.cap // 16 * 16
        self.tail = self.cap - self.main
        self.parts = 16 // self.tail if self.tail else 0
        self.per_part = -(-self.chunks // self.parts) if self.tail else 0
        self.slot_rows = self.chunks * self.main + 16 * self.per_part
        first = -(-(self.kw // 128) // 2) * 128
        self.cols = (pl.ds(0, first), pl.ds(first, self.kw - first))


def kernel(
    p,
    limit_ref, owners_ref, routes_ref, feat_ref, prelat_ref, prerope_ref, spanlat_ref, spanrope_ref,
    qlat_hbm, qrope_hbm, gate_hbm, up_hbm,
    att_ref, hidden_ref, miglat_ref, migrope_ref,
    qlat, qrope, gate, up, kv, slots, outgoing, bias, assembled,
    local_sem, kvz_s, kvz_r, kvc_s, kvc_r, sz_s, sz_r, sx_s, sx_r, sc_s, sc_r,
):
    n, nx = p.n, p.nx
    me = lax.axis_index("expert")
    head = lax.axis_index("head")
    core = lax.rem(head, 2)
    xpos = lax.div(head, 2)
    partner = head + 1 - 2 * core

    def z_to(k):
        return lax.rem(me - k + n, n)

    def z_from(k):
        return lax.rem(me + k, n)

    def x_to(j):
        return lax.rem(xpos - j + nx, nx) * 2 + core

    def x_from(j):
        return lax.rem(xpos + j, nx) * 2 + core

    barrier = pltpu.get_barrier_semaphore()
    each_from(1, n, lambda k: pl.semaphore_signal(
        barrier, inc=1, device_id={"expert": z_to(k)}, device_id_type=MESH))
    each_from(1, nx, lambda j: pl.semaphore_signal(
        barrier, inc=1, device_id={"head": x_to(j)}, device_id_type=MESH))
    pl.semaphore_signal(barrier, inc=1, device_id={"head": partner}, device_id_type=MESH)

    loads = [
        pltpu.make_async_copy(src, dst, local_sem.at[i])
        for i, (src, dst) in enumerate(
            ((qlat_hbm, qlat), (qrope_hbm, qrope), (gate_hbm.at[0], gate), (up_hbm.at[0], up)))
    ]
    for load in loads:
        load.start()

    limit = limit_ref[0]
    prefix_pos = me * p.pre + lax.broadcasted_iota(jnp.int32, (p.pre, 1), 0)
    kept = prefix_pos < limit
    zero_pad = jnp.zeros((p.pre, p.rope), jnp.float32)
    kv[me, 0:p.pre, 0:p.lat] = jnp.where(
        kept, prelat_ref[...].astype(jnp.float32), 0.0).astype(jnp.bfloat16)
    kv[me, p.pre:p.block, 0:p.lat] = spanlat_ref[...]
    kv[me, 0:p.pre, p.lat:p.kw] = jnp.concatenate(
        [jnp.where(kept, prerope_ref[...].astype(jnp.float32), 0.0), zero_pad], axis=1
    ).astype(jnp.bfloat16)
    kv[me, p.pre:p.block, p.lat:p.kw] = jnp.concatenate(
        [spanrope_ref[...], jnp.zeros((p.tok, p.rope), jnp.bfloat16)], axis=1)

    feats = feat_ref[...]
    older = (lax.broadcasted_iota(jnp.int32, (p.tok, p.tok), 0)
             <= lax.broadcasted_iota(jnp.int32, (p.tok, p.tok), 1))
    older = older.astype(jnp.float32).astype(jnp.bfloat16)
    sel_rows = p.main + (16 if p.tail else 0)
    row = lax.broadcasted_iota(jnp.int32, (sel_rows, p.tok), 0)
    slot_id = row
    if p.tail:
        for q in range(1, p.parts):
            slot_id = slot_id - jnp.where(row >= p.main + q * p.tail, p.tail, 0)
    slot_id = slot_id.astype(jnp.float32)

    def slot_values(expert, put):
        named = jnp.zeros((1, p.tok), jnp.float32)
        for t in range(p.top):
            named = jnp.maximum(named, (routes_ref[t:t + 1, :] == expert).astype(jnp.float32))
        named8 = jnp.broadcast_to(named, (16, p.tok))
        rank = jnp.dot(named8.astype(jnp.bfloat16), older, preferred_element_type=jnp.float32) - 1.0
        rank = jnp.where(named8 > 0.5, rank, -1.0)[0:1, :]
        chosen = (rank == slot_id).astype(jnp.float32).astype(jnp.bfloat16)
        picked = jnp.dot(chosen, feats, preferred_element_type=jnp.float32)
        for c in range(p.chunks):
            put(c * p.main, p.main,
                picked[0:p.main, c * p.cw:(c + 1) * p.cw].astype(jnp.bfloat16))
        if p.tail:
            trow = lax.broadcasted_iota(jnp.int32, (16, p.cw), 0)
            for part in range(p.per_part):
                value = jnp.zeros((16, p.cw), jnp.float32)
                for q in range(p.parts):
                    c = q * p.per_part + part
                    if c < p.chunks:
                        inside = (trow >= q * p.tail) & (trow < (q + 1) * p.tail)
                        value = jnp.where(
                            inside, picked[p.main:sel_rows, c * p.cw:(c + 1) * p.cw], value)
                put(p.chunks * p.main + 16 * part, 16, value.astype(jnp.bfloat16))

    def fill(k):
        def put(at, rows, value):
            outgoing[k, at:at + rows, :] = value
        slot_values(z_to(k), put)

    def fill_own():
        def put(at, rows, value):
            slots[head, me, at:at + rows, :] = value
        slot_values(me, put)

    def kv_z(k, c):
        return pltpu.make_async_remote_copy(
            src_ref=kv.at[me, :, p.cols[c]], dst_ref=kv.at[me, :, p.cols[c]],
            send_sem=kvz_s.at[k], recv_sem=kvz_r.at[k],
            device_id={"expert": z_to(k)}, device_id_type=MESH)

    def kv_z_in(k, c):
        src = z_from(k)
        return pltpu.make_async_remote_copy(
            src_ref=kv.at[src, :, p.cols[c]], dst_ref=kv.at[src, :, p.cols[c]],
            send_sem=kvz_s.at[k], recv_sem=kvz_r.at[k],
            device_id={"expert": z_to(k)}, device_id_type=MESH)

    def kv_c(k, c):
        src = z_from(k)
        return pltpu.make_async_remote_copy(
            src_ref=kv.at[src, :, p.cols[c]], dst_ref=kv.at[src, :, p.cols[c]],
            send_sem=kvc_s.at[k], recv_sem=kvc_r.at[k],
            device_id={"head": partner}, device_id_type=MESH)

    def slot_z(k):
        return pltpu.make_async_remote_copy(
            src_ref=outgoing.at[k], dst_ref=slots.at[head, me],
            send_sem=sz_s.at[k], recv_sem=sz_r.at[k],
            device_id={"expert": z_to(k)}, device_id_type=MESH)

    def slot_z_in(k):
        return pltpu.make_async_remote_copy(
            src_ref=outgoing.at[k], dst_ref=slots.at[head, z_from(k)],
            send_sem=sz_s.at[k], recv_sem=sz_r.at[k],
            device_id={"expert": z_to(k)}, device_id_type=MESH)

    def slot_x(j, k, whose):
        ref = slots.at[whose, z_from(k)]
        return pltpu.make_async_remote_copy(
            src_ref=ref, dst_ref=ref, send_sem=sx_s.at[j, k], recv_sem=sx_r.at[j, k],
            device_id={"head": x_to(j)}, device_id_type=MESH)

    def slot_c(j, k, whose):
        ref = slots.at[whose, z_from(k)]
        return pltpu.make_async_remote_copy(
            src_ref=ref, dst_ref=ref, send_sem=sc_s.at[j, k], recv_sem=sc_r.at[j, k],
            device_id={"head": partner}, device_id_type=MESH)

    def by_core(step):
        for c in (0, 1):
            pl.when(core == c)(functools.partial(step, c))

    def forward_own(k):
        each_from(1, nx, lambda j: slot_x(j, k, head).start())
        slot_c(0, k, head).start()

    def forward_x(k):
        def one(j):
            slot_x(j, k, x_from(j)).wait_recv()
            slot_c(j, k, x_from(j)).start()
        each_from(1, nx, one)

    each_from(1, n, fill)
    fill_own()

    pl.semaphore_wait(barrier, n - 1 + nx - 1 + 1)

    by_core(lambda c: each_from(1, n, lambda k: kv_z(k, c).start()))
    each_from(1, n, lambda k: slot_z(k).start())
    forward_own(0)

    col = lax.broadcasted_iota(jnp.int32, (p.tok, p.keys), 1).astype(jnp.float32)
    query = (me * p.tok + lax.broadcasted_iota(jnp.int32, (p.tok, p.keys), 0)).astype(jnp.float32)
    source = jnp.floor((col + 0.5) * (1.0 / p.block))
    within = col - source * p.block
    in_prefix = within < p.pre
    reach = jnp.where(in_prefix, limit.astype(jnp.float32) - 1.0, query)
    place = jnp.where(in_prefix, source * p.pre + within, source * p.tok + within - p.pre)
    bias[...] = jnp.where(place <= reach, 0.0, -1e30)

    def kv_forward(c):
        def one(k):
            kv_z_in(k, c).wait_recv()
            kv_c(k, c).start()
        each_from(1, n, one)

    def kv_take(c):
        each_from(1, n, lambda k: kv_c(k, 1 - c).wait_recv())

    by_core(kv_forward)
    by_core(kv_take)
    loads[0].wait()
    loads[1].wait()

    group = 4 if p.heads % 4 == 0 else 2
    pairs = group // 2

    def attend(g):
        keys = kv[...].reshape(p.keys, p.kw)
        values = keys[:, 0:p.lat]
        rope_even = keys[:, p.lat:p.kw]
        rope_odd = jnp.concatenate([rope_even[:, p.rope:], rope_even[:, :p.rope]], axis=1)
        order = list(range(0, group, 2)) + list(range(1, group, 2))

        def lat_at(h):
            return pl.ds(pl.multiple_of((g * group + h) * p.lat, 128), p.lat)

        q_lat = jnp.concatenate([qlat[:, lat_at(h)] for h in order], axis=0)
        q_rot = jnp.concatenate(
            [qrope[:, pl.ds(pl.multiple_of((g * pairs + i) * 2 * p.rope, 128), 2 * p.rope)]
             for i in range(pairs)], axis=0)
        scores = lax.dot_general(q_lat, values, NT, preferred_element_type=jnp.float32)
        rot = jnp.concatenate(
            [lax.dot_general(q_rot, rope_even, NT, preferred_element_type=jnp.float32),
             lax.dot_general(q_rot, rope_odd, NT, preferred_element_type=jnp.float32)], axis=0)
        shown = (scores + rot) * SOFTMAX_SCALE + jnp.concatenate([bias[...]] * group, axis=0)
        weights = jnp.exp(shown - jnp.max(shown, axis=1, keepdims=True))
        total = jnp.sum(weights, axis=1, keepdims=True)
        mixed = jnp.dot(weights.astype(jnp.bfloat16), values, preferred_element_type=jnp.float32)
        result = (mixed / total).astype(jnp.bfloat16)
        for i, h in enumerate(order):
            att_ref[:, lat_at(h)] = result[i * p.tok:(i + 1) * p.tok, :]

    steps = p.heads // group
    done = 0
    for k in range(1, n) if n <= 4 else []:
        slot_z_in(k).wait_recv()
        forward_own(k)
        forward_x(k - 1)
        upto = steps * k // (n - 1)
        if upto > done:
            lax.fori_loop(done, upto, lambda g, carry: (attend(g), carry)[1], 0)
        done = upto
    if n > 4:
        def many(k):
            slot_z_in(k).wait_recv()
            forward_own(k)
            forward_x(k - 1)
        each_from(1, n, many)
        lax.fori_loop(0, steps, lambda g, carry: (attend(g), carry)[1], 0)

    mine = jnp.int32(0)
    for s in range(n):
        mine = jnp.where(owners_ref[s] == me, s, mine)
    block = kv[mine]
    miglat_ref[...] = block[:, 0:p.lat]
    migrope_ref[...] = block[:, p.lat:p.lat + p.rope]

    loads[2].wait()
    loads[3].wait()
    rows_main, rows_tail = n * p.main, 16 * n if p.tail else 0
    tail_row = lax.broadcasted_iota(jnp.int32, (n, 16, p.cw), 1)

    def expert_part(which, totals):
        gated, upward = totals
        for c in range(p.chunks):
            lhs = slots[which, :, c * p.main:(c + 1) * p.main, :].reshape(rows_main, p.cw)
            if p.tail:
                q, part = c // p.per_part, c % p.per_part
                at = p.chunks * p.main + 16 * part
                extra = slots[which, :, at:at + 16, :].astype(jnp.float32)
                inside = (tail_row >= q * p.tail) & (tail_row < (q + 1) * p.tail)
                extra = jnp.where(inside, extra, 0.0).astype(jnp.bfloat16)
                lhs = jnp.concatenate([lhs, extra.reshape(rows_tail, p.cw)], axis=0)
            at = pl.ds(pl.multiple_of(which * p.width + c * p.cw, 128), p.cw)
            gated = gated + jnp.dot(lhs, gate[at, :], preferred_element_type=jnp.float32)
            upward = upward + jnp.dot(lhs, up[at, :], preferred_element_type=jnp.float32)
        return gated, upward

    zero = jnp.zeros((rows_main + rows_tail, p.hidden), jnp.float32)
    totals = expert_part(head, (zero, zero))
    each(n, lambda k: slot_c(0, k, partner).wait_recv())
    totals = expert_part(partner, totals)
    forward_x(n - 1)
    for j in range(1, nx):
        totals = expert_part(x_from(j), totals)
    for j in range(1, nx):
        whose = x_from(j) + 1 - 2 * core
        each(n, lambda k: slot_c(j, k, whose).wait_recv())
        totals = expert_part(whose, totals)
    gated, upward = totals

    def finish(g, u):
        return g / (1.0 + jnp.exp(-g)) * u

    for s in range(n):
        at = slice(s * p.main, (s + 1) * p.main)
        assembled[s * p.cap:s * p.cap + p.main, :] = finish(gated[at, :], upward[at, :])
        if p.tail:
            g = jnp.zeros((p.tail, p.hidden), jnp.float32)
            u = g
            for q in range(p.parts):
                at = rows_main + 16 * s + q * p.tail
                g = g + gated[at:at + p.tail, :]
                u = u + upward[at:at + p.tail, :]
            assembled[s * p.cap + p.main:(s + 1) * p.cap, :] = finish(g, u)
    hidden_ref[0] = assembled[...].astype(jnp.bfloat16)

    by_core(lambda c: each_from(1, n, lambda k: kv_z(k, c).wait_send()))
    by_core(lambda c: each_from(1, n, lambda k: kv_c(k, c).wait_send()))
    each_from(1, n, lambda k: slot_z(k).wait_send())

    def sent(k):
        each_from(1, nx, lambda j: slot_x(j, k, head).wait_send())
        slot_c(0, k, head).wait_send()
        each_from(1, nx, lambda j: slot_c(j, k, x_from(j)).wait_send())
    each(n, sent)


def body(
    q_latent, q_rope, prefix_latent, prefix_rope, span_latent, span_rope,
    prefix_len, moe_input, routes, owners, gate_weight, up_weight,
):
    n = lax.axis_size("expert")
    nh = lax.axis_size("head")
    rope = span_rope.shape[1]
    p = Plan(
        n, nh, span_latent.shape[0], prefix_latent.shape[0], span_latent.shape[1], rope,
        q_rope.shape[1] // rope, moe_input.shape[1], routes.shape[1], gate_weight.shape[2])
    bf16, f32 = jnp.bfloat16, jnp.float32
    vmem = pl.BlockSpec(memory_space=pltpu.VMEM)
    smem = pl.BlockSpec(memory_space=pltpu.SMEM)
    hbm = pl.BlockSpec(memory_space=pl.ANY)
    dma = pltpu.SemaphoreType.DMA
    return pl.pallas_call(
        functools.partial(kernel, p),
        out_shape=(
            jax.ShapeDtypeStruct(q_latent.shape, bf16),
            jax.ShapeDtypeStruct((1, n * p.cap, p.hidden), bf16),
            jax.ShapeDtypeStruct((p.block, p.lat), bf16),
            jax.ShapeDtypeStruct((p.block, p.rope), bf16),
        ),
        in_specs=[smem, smem] + [vmem] * 6 + [hbm] * 4,
        out_specs=(vmem,) * 4,
        scratch_shapes=[
            pltpu.VMEM(q_latent.shape, bf16),
            pltpu.VMEM(q_rope.shape, bf16),
            pltpu.VMEM(gate_weight.shape[1:], bf16),
            pltpu.VMEM(up_weight.shape[1:], bf16),
            pltpu.VMEM((n, p.block, p.kw), bf16),
            pltpu.VMEM((nh, n, p.slot_rows, p.cw), bf16),
            pltpu.VMEM((n, p.slot_rows, p.cw), bf16),
            pltpu.VMEM((p.tok, p.keys), f32),
            pltpu.VMEM((n * p.cap, p.hidden), f32),
            dma((4,)),
            dma((n,)), dma((n,)), dma((n,)), dma((n,)), dma((n,)), dma((n,)),
            dma((p.nx, n)), dma((p.nx, n)), dma((p.nx, n)), dma((p.nx, n)),
        ],
        compiler_params=pltpu.CompilerParams(
            collective_id=0, has_side_effects=True, vmem_limit_bytes=56 * 1024 * 1024),
    )(prefix_len, owners, routes.T, moe_input, prefix_latent, prefix_rope, span_latent, span_rope,
      q_latent, q_rope, gate_weight, up_weight)


def solution(mesh):
    in_specs = (
        P(("group", "expert"), "head"),
        P(("group", "expert"), "head"),
        P(("group", "expert"), None),
        P(("group", "expert"), None),
        P(("group", "expert"), None),
        P(("group", "expert"), None),
        P("group"),
        P(("group", "expert"), "head"),
        P(("group", "expert"), None),
        P("group"),
        P("expert", None, "head"),
        P("expert", None, "head"),
    )
    out_specs = (
        P(("group", "expert"), "head"),
        P(("group", "expert"), None, "head"),
        P(("group", "expert"), None),
        P(("group", "expert"), None),
    )
    return jax.shard_map(body, mesh=mesh, in_specs=in_specs, out_specs=out_specs, check_vma=False)
```

time: 130 us -> 41.2 us (0.32)
  the two profiles are of different devices: /device:TPU:0 before, /device:TPU:1 now
where the time goes in v1:
time: 41.2 us; the launch traced here: 40.9 us
  Pallas kernels  32.9 us (80%)
  local copies, waits for them, and re-layouts  6.73 us (16%)
  between operations  1.29 us (3%)
    pallas_call x1, Pallas kernels, body(): pl.pallas_call(functools.partial(kernel, p), out_shape=(jax.ShapeDtypeStr...  32.9 us
    unnamed x3, local copies, waits for them, and re-layouts  5.31 us
    pallas_call x1, local copies, waits for them, and re-layouts, body(): pl.pallas_call(functools.partial(kernel, p), out_shape=(jax.ShapeDtypeStr...  1.42 us

profile of v1, /device:TPU:1, one launch (start us, length us, event | category | flops | bytes accessed | tf_op | source)
XLA Modules:
  0.0 40.9 jit_solution(3694476321611907624)
XLA Ops:
  1.3 32.9 %shard_map.147 = (bf16[64,8192]{1,0:T(8,128)(2,1)}, bf16[1,144,256]{2,1,0:T(8,128)(2,1)}, bf16[80,512]{1,0:T(8,128)(2,1)}, bf16[80,64]{1,0:T(8,128)(2,1)}) custom-call(s32[1]{0:T(128)S(6)} %copy.20.limit_ref, s32[4]{0:T(128)} %owners_ref.1, s32[2,64]{1,0:T(2,128)} %bitcast.1, bf16[64,1792]{1,0:T(8,128)(2,1)} %feat_ref.1, bf16[16,512]{1,0:T(8,128)(2,1)} %prelat_ref.1, ...), custom_call_target="tpu_custom_call" | custom-call | tf_op jit(solution)/shard_map/pallas_call | solution.py:371
  34.2 1.4 %copy.16 = bf16[80,64]{0,1:T(8,128)(2,1)} copy(bf16[80,64]{1,0:T(8,128)(2,1)} %get-tuple-element.7) | data formatting | bytes 20480 | tf_op jit(solution)/shard_map/pallas_call | solution.py:371
  35.6 2.3 %copy.21 = bf16[64,8192]{1,0:T(8,128)(2,1)} copy(bf16[64,8192]{1,0:T(8,128)(2,1)} %get-tuple-element.12) | data formatting | bytes 2097152
  37.9 1.5 %copy.22 = bf16[1,144,256]{2,1,0:T(8,128)(2,1)} copy(bf16[1,144,256]{2,1,0:T(8,128)(2,1)} %get-tuple-element.13) | data formatting | bytes 147456
  39.4 1.5 %copy.23 = bf16[80,512]{1,0:T(8,128)(2,1)} copy(bf16[80,512]{1,0:T(8,128)(2,1)} %get-tuple-element.14) | data formatting | bytes 163840

commit v2 on v1

--- a/solution.py
+++ b/solution.py
@@ -10,6 +10,9 @@
 SOFTMAX_SCALE = 192.0 ** (-0.5)
 MESH = pl.DeviceIdType.MESH
 NT = (((1,), (1,)), ((), ()))
+AHEAD = 3
+KV_AT = 0
+KV_USE = 2
 
 
 def each(count, step):
@@ -43,8 +46,18 @@
         self.parts = 16 // self.tail if self.tail else 0
         self.per_part = -(-self.chunks // self.parts) if self.tail else 0
         self.slot_rows = self.chunks * self.main + 16 * self.per_part
+        self.halves = 2 if self.slot_rows % 32 == 0 else 1
         first = -(-(self.kw // 128) // 2) * 128
         self.cols = (pl.ds(0, first), pl.ds(first, self.kw - first))
+        tiles, self.rows, at = self.block // 16, [], 0
+        for x in range(self.nx):
+            count = tiles // self.nx + (1 if x < tiles % self.nx else 0)
+            self.rows.append(pl.ds(at * 16, count * 16) if count else None)
+            at += count
+
+    def piece(self, h):
+        rows = self.rows[h // 2]
+        return None if rows is None else (rows, self.cols[h % 2])
 
 
 def kernel(
@@ -53,7 +66,7 @@
     qlat_hbm, qrope_hbm, gate_hbm, up_hbm,
     att_ref, hidden_ref, miglat_ref, migrope_ref,
     qlat, qrope, gate, up, kv, slots, outgoing, bias, assembled,
-    local_sem, kvz_s, kvz_r, kvc_s, kvc_r, sz_s, sz_r, sx_s, sx_r, sc_s, sc_r,
+    local_sem, kvz_s, kvz_r, kvx_s, kvx_r, kvc_s, kvc_r, sz_s, sz_r, sx_s, sx_r, sc_s, sc_r,
 ):
     n, nx = p.n, p.nx
     me = lax.axis_index("expert")
@@ -148,72 +161,134 @@
             slots[head, me, at:at + rows, :] = value
         slot_values(me, put)
 
-    def kv_z(k, c):
+    def kv_copy(h, k, sems, target):
+        rows, cols = p.piece(h)
+        ref = kv.at[z_from(k), rows, cols]
         return pltpu.make_async_remote_copy(
-            src_ref=kv.at[me, :, p.cols[c]], dst_ref=kv.at[me, :, p.cols[c]],
-            send_sem=kvz_s.at[k], recv_sem=kvz_r.at[k],
+            src_ref=ref, dst_ref=ref, send_sem=sems[0], recv_sem=sems[1],
+            device_id=target, device_id_type=MESH)
+
+    def kv_z(h, k):
+        rows, cols = p.piece(h)
+        ref = kv.at[me, rows, cols]
+        return pltpu.make_async_remote_copy(
+            src_ref=ref, dst_ref=ref, send_sem=kvz_s.at[k], recv_sem=kvz_r.at[k],
             device_id={"expert": z_to(k)}, device_id_type=MESH)
 
-    def kv_z_in(k, c):
-        src = z_from(k)
+    def kv_z_in(h, k):
+        return kv_copy(h, k, (kvz_s.at[k], kvz_r.at[k]), {"expert": z_to(k)})
+
+    def kv_x(h, j, k):
+        return kv_copy(h, k, (kvx_s.at[j, k], kvx_r.at[j, k]), {"head": x_to(j)})
+
+    def kv_c(h, j, k):
+        return kv_copy(h, k, (kvc_s.at[j, k], kvc_r.at[j, k]), {"head": partner})
+
+    def by_head(step):
+        for h in range(p.nh):
+            def at(j, c):
+                return ((h // 2 + j) % nx) * 2 + c
+            along = [(j, at(j, h % 2)) for j in range(1, nx) if p.piece(at(j, 0))]
+            across = [(j, at(j, 1 - h % 2)) for j in range(nx) if p.piece(at(j, 0))]
+            pl.when(head == h)(functools.partial(step, h, p.piece(h) is not None, along, across))
+
+    part_rows = p.slot_rows // p.halves
+
+    def part_of(i):
+        return pl.ds(i * part_rows, part_rows)
+
+    def slot_z(k, i):
         return pltpu.make_async_remote_copy(
-            src_ref=kv.at[src, :, p.cols[c]], dst_ref=kv.at[src, :, p.cols[c]],
-            send_sem=kvz_s.at[k], recv_sem=kvz_r.at[k],
+            src_ref=outgoing.at[k, part_of(i)], dst_ref=slots.at[head, me, part_of(i)],
+            send_sem=sz_s.at[k, i], recv_sem=sz_r.at[k, i],
             device_id={"expert": z_to(k)}, device_id_type=MESH)
 
-    def kv_c(k, c):
-        src = z_from(k)
+    def slot_z_in(k, i):
         return pltpu.make_async_remote_copy(
-            src_ref=kv.at[src, :, p.cols[c]], dst_ref=kv.at[src, :, p.cols[c]],
-            send_sem=kvc_s.at[k], recv_sem=kvc_r.at[k],
+            src_ref=outgoing.at[k, part_of(i)], dst_ref=slots.at[head, z_from(k), part_of(i)],
+            send_sem=sz_s.at[k, i], recv_sem=sz_r.at[k, i],
+            device_id={"expert": z_to(k)}, device_id_type=MESH)
+
+    def slot_x(j, k, i, whose):
+        ref = slots.at[whose, z_from(k), part_of(i)]
+        return pltpu.make_async_remote_copy(
+            src_ref=ref, dst_ref=ref, send_sem=sx_s.at[j, k, i], recv_sem=sx_r.at[j, k, i],
+            device_id={"head": x_to(j)}, device_id_type=MESH)
+
+    def slot_c(j, k, i, whose):
+        ref = slots.at[whose, z_from(k), part_of(i)]
+        return pltpu.make_async_remote_copy(
+            src_ref=ref, dst_ref=ref, send_sem=sc_s.at[j, k, i], recv_sem=sc_r.at[j, k, i],
             device_id={"head": partner}, device_id_type=MESH)
 
-    def slot_z(k):
-        return pltpu.make_async_remote_copy(
-            src_ref=outgoing.at[k], dst_ref=slots.at[head, me],
-            send_sem=sz_s.at[k], recv_sem=sz_r.at[k],
-            device_id={"expert": z_to(k)}, device_id_type=MESH)
-
-    def slot_z_in(k):
-        return pltpu.make_async_remote_copy(
-            src_ref=outgoing.at[k], dst_ref=slots.at[head, z_from(k)],
-            send_sem=sz_s.at[k], recv_sem=sz_r.at[k],
-            device_id={"expert": z_to(k)}, device_id_type=MESH)
-
-    def slot_x(j, k, whose):
-        ref = slots.at[whose, z_from(k)]
-        return pltpu.make_async_remote_copy(
-            src_ref=ref, dst_ref=ref, send_sem=sx_s.at[j, k], recv_sem=sx_r.at[j, k],
-            device_id={"head": x_to(j)}, device_id_type=MESH)
-
-    def slot_c(j, k, whose):
-        ref = slots.at[whose, z_from(k)]
-        return pltpu.make_async_remote_copy(
-            src_ref=ref, dst_ref=ref, send_sem=sc_s.at[j, k], recv_sem=sc_r.at[j, k],
-            device_id={"head": partner}, device_id_type=MESH)
-
-    def by_core(step):
-        for c in (0, 1):
-            pl.when(core == c)(functools.partial(step, c))
-
-    def forward_own(k):
-        each_from(1, nx, lambda j: slot_x(j, k, head).start())
-        slot_c(0, k, head).start()
-
-    def forward_x(k):
+    def forward_own(k, i):
+        each_from(1, nx, lambda j: slot_x(j, k, i, head).start())
+        slot_c(0, k, i, head).start()
+
+    def forward_x(k, i):
         def one(j):
-            slot_x(j, k, x_from(j)).wait_recv()
-            slot_c(j, k, x_from(j)).start()
+            slot_x(j, k, i, x_from(j)).wait_recv()
+            slot_c(j, k, i, x_from(j)).start()
         each_from(1, nx, one)
+
+    def each_part(step):
+        for i in range(p.halves):
+            step(i)
 
     each_from(1, n, fill)
     fill_own()
 
     pl.semaphore_wait(barrier, n - 1 + nx - 1 + 1)
 
-    by_core(lambda c: each_from(1, n, lambda k: kv_z(k, c).start()))
-    each_from(1, n, lambda k: slot_z(k).start())
-    forward_own(0)
+    def kv_first(h, own, along, across):
+        if own:
+            each_from(1, n, lambda k: kv_z(h, k).start())
+
+    def kv_forward(h, own, along, across):
+        def one(k):
+            kv_z_in(h, k).wait_recv()
+            for j in range(1, nx):
+                kv_x(h, j, k).start()
+            kv_c(h, 0, k).start()
+        if own:
+            each_from(1, n, one)
+
+    def kv_onward(h, own, along, across):
+        def one(k):
+            for j, other in along:
+                kv_x(other, j, k).wait_recv()
+                kv_c(other, j, k).start()
+        each_from(1, n, one)
+
+    def kv_take(h, own, along, across):
+        def one(k):
+            for j, other in across:
+                kv_c(other, j, k).wait_recv()
+        each_from(1, n, one)
+
+    def kv_sent(h, own, along, across):
+        def one(k):
+            if own:
+                kv_z(h, k).wait_send()
+                for j in range(1, nx):
+                    kv_x(h, j, k).wait_send()
+                kv_c(h, 0, k).wait_send()
+            for j, other in along:
+                kv_c(other, j, k).wait_send()
+        each_from(1, n, one)
+
+    units = [(k, i) for k in range(1, n) for i in range(p.halves)]
+    ahead = AHEAD if n <= 4 else len(units)
+    if KV_AT == 0:
+        by_head(kv_first)
+    each_part(lambda i: forward_own(0, i))
+    if n <= 4:
+        for k, i in units[:ahead]:
+            slot_z(k, i).start()
+    else:
+        each_part(lambda i: each_from(1, n, lambda k: slot_z(k, i).start()))
+    if KV_AT == 1:
+        by_head(kv_first)
 
     col = lax.broadcasted_iota(jnp.int32, (p.tok, p.keys), 1).astype(jnp.float32)
     query = (me * p.tok + lax.broadcasted_iota(jnp.int32, (p.tok, p.keys), 0)).astype(jnp.float32)
@@ -224,19 +299,6 @@
     place = jnp.where(in_prefix, source * p.pre + within, source * p.tok + within - p.pre)
     bias[...] = jnp.where(place <= reach, 0.0, -1e30)
 
-    def kv_forward(c):
-        def one(k):
-            kv_z_in(k, c).wait_recv()
-            kv_c(k, c).start()
-        each_from(1, n, one)
-
-    def kv_take(c):
-        each_from(1, n, lambda k: kv_c(k, 1 - c).wait_recv())
-
-    by_core(kv_forward)
-    by_core(kv_take)
-    loads[0].wait()
-    loads[1].wait()
 
     group = 4 if p.heads % 4 == 0 else 2
     pairs = group // 2
@@ -268,29 +330,56 @@
             att_ref[:, lat_at(h)] = result[i * p.tok:(i + 1) * p.tok, :]
 
     steps = p.heads // group
-    done = 0
-    for k in range(1, n) if n <= 4 else []:
-        slot_z_in(k).wait_recv()
-        forward_own(k)
-        forward_x(k - 1)
-        upto = steps * k // (n - 1)
-        if upto > done:
-            lax.fori_loop(done, upto, lambda g, carry: (attend(g), carry)[1], 0)
-        done = upto
-    if n > 4:
+
+    def attend_all(first, last):
+        lax.fori_loop(first, last, lambda g, carry: (attend(g), carry)[1], 0)
+
+    def kv_gathered():
+        by_head(kv_forward)
+        by_head(kv_onward)
+        by_head(kv_take)
+        loads[0].wait()
+        loads[1].wait()
+
+    if n <= 4:
+        before = [(0, i) for i in range(p.halves)]
+        started = 0
+        for at, (k, i) in enumerate(units):
+            if at == KV_USE:
+                kv_gathered()
+                started = at
+            slot_z_in(k, i).wait_recv()
+            forward_own(k, i)
+            if at + ahead < len(units):
+                slot_z(*units[at + ahead]).start()
+            forward_x(*before[0])
+            before = before[1:] + [(k, i)]
+            if at >= KV_USE:
+                span = len(units) - KV_USE
+                first, last = (steps * (at - KV_USE + d) // span for d in (0, 1))
+                if last > first:
+                    attend_all(first, last)
+    else:
+        kv_gathered()
+        each_part(lambda i: forward_x(0, i))
+
         def many(k):
-            slot_z_in(k).wait_recv()
-            forward_own(k)
-            forward_x(k - 1)
+            def one(i):
+                slot_z_in(k, i).wait_recv()
+                forward_own(k, i)
+            each_part(one)
         each_from(1, n, many)
-        lax.fori_loop(0, steps, lambda g, carry: (attend(g), carry)[1], 0)
+        before = [(n - 1, i) for i in range(p.halves)]
+        each_part(lambda i: each_from(1, n - 1, lambda k: forward_x(k, i)))
+        attend_all(0, steps)
 
     mine = jnp.int32(0)
     for s in range(n):
         mine = jnp.where(owners_ref[s] == me, s, mine)
     block = kv[mine]
     miglat_ref[...] = block[:, 0:p.lat]
-    migrope_ref[...] = block[:, p.lat:p.lat + p.rope]
+    turned = jnp.transpose(block[:, p.lat:p.kw].astype(jnp.float32))
+    migrope_ref[...] = turned[0:p.rope, :].astype(jnp.bfloat16)
 
     loads[2].wait()
     loads[3].wait()
@@ -315,14 +404,15 @@
 
     zero = jnp.zeros((rows_main + rows_tail, p.hidden), jnp.float32)
     totals = expert_part(head, (zero, zero))
-    each(n, lambda k: slot_c(0, k, partner).wait_recv())
+    each_part(lambda i: each(n, lambda k: slot_c(0, k, i, partner).wait_recv()))
     totals = expert_part(partner, totals)
-    forward_x(n - 1)
+    for k, i in before:
+        forward_x(k, i)
     for j in range(1, nx):
         totals = expert_part(x_from(j), totals)
     for j in range(1, nx):
         whose = x_from(j) + 1 - 2 * core
-        each(n, lambda k: slot_c(j, k, whose).wait_recv())
+        each_part(lambda i: each(n, lambda k: slot_c(j, k, i, whose).wait_recv()))
         totals = expert_part(whose, totals)
     gated, upward = totals
 
@@ -342,15 +432,32 @@
             assembled[s * p.cap + p.main:(s + 1) * p.cap, :] = finish(g, u)
     hidden_ref[0] = assembled[...].astype(jnp.bfloat16)
 
-    by_core(lambda c: each_from(1, n, lambda k: kv_z(k, c).wait_send()))
-    by_core(lambda c: each_from(1, n, lambda k: kv_c(k, c).wait_send()))
-    each_from(1, n, lambda k: slot_z(k).wait_send())
+    by_head(kv_sent)
+    each_part(lambda i: each_from(1, n, lambda k: slot_z(k, i).wait_send()))
 
     def sent(k):
-        each_from(1, nx, lambda j: slot_x(j, k, head).wait_send())
-        slot_c(0, k, head).wait_send()
-        each_from(1, nx, lambda j: slot_c(j, k, x_from(j)).wait_send())
+        def one(i):
+            each_from(1, nx, lambda j: slot_x(j, k, i, head).wait_send())
+            slot_c(0, k, i, head).wait_send()
+            each_from(1, nx, lambda j: slot_c(j, k, i, x_from(j)).wait_send())
+        each_part(one)
     each(n, sent)
+
+
+def place_kernel(count, *refs):
+    sources, targets = refs[:count], refs[count:2 * count]
+    held, in_sem, out_sem = refs[2 * count:3 * count], refs[3 * count], refs[3 * count + 1]
+    ins = [pltpu.make_async_copy(a, b, in_sem.at[i])
+           for i, (a, b) in enumerate(zip(sources, held))]
+    outs = [pltpu.make_async_copy(a, b, out_sem.at[i])
+            for i, (a, b) in enumerate(zip(held, targets))]
+    for copy in ins:
+        copy.start()
+    for i in range(count):
+        ins[i].wait()
+        outs[i].start()
+    for copy in outs:
+        copy.wait()
 
 
 def body(
@@ -368,13 +475,13 @@
     smem = pl.BlockSpec(memory_space=pltpu.SMEM)
     hbm = pl.BlockSpec(memory_space=pl.ANY)
     dma = pltpu.SemaphoreType.DMA
-    return pl.pallas_call(
+    results = pl.pallas_call(
         functools.partial(kernel, p),
         out_shape=(
             jax.ShapeDtypeStruct(q_latent.shape, bf16),
             jax.ShapeDtypeStruct((1, n * p.cap, p.hidden), bf16),
             jax.ShapeDtypeStruct((p.block, p.lat), bf16),
-            jax.ShapeDtypeStruct((p.block, p.rope), bf16),
+            jax.ShapeDtypeStruct((p.rope, p.block), bf16),
         ),
         in_specs=[smem, smem] + [vmem] * 6 + [hbm] * 4,
         out_specs=(vmem,) * 4,
@@ -389,13 +496,23 @@
             pltpu.VMEM((p.tok, p.keys), f32),
             pltpu.VMEM((n * p.cap, p.hidden), f32),
             dma((4,)),
-            dma((n,)), dma((n,)), dma((n,)), dma((n,)), dma((n,)), dma((n,)),
-            dma((p.nx, n)), dma((p.nx, n)), dma((p.nx, n)), dma((p.nx, n)),
+            dma((n,)), dma((n,)), dma((p.nx, n)), dma((p.nx, n)), dma((p.nx, n)), dma((p.nx, n)),
+            dma((n, p.halves)), dma((n, p.halves)),
+            dma((p.nx, n, p.halves)), dma((p.nx, n, p.halves)),
+            dma((p.nx, n, p.halves)), dma((p.nx, n, p.halves)),
         ],
         compiler_params=pltpu.CompilerParams(
             collective_id=0, has_side_effects=True, vmem_limit_bytes=56 * 1024 * 1024),
     )(prefix_len, owners, routes.T, moe_input, prefix_latent, prefix_rope, span_latent, span_rope,
       q_latent, q_rope, gate_weight, up_weight)
+    attended, hidden, mig_lat, mig_rope = pl.pallas_call(
+        functools.partial(place_kernel, 4),
+        out_shape=[jax.ShapeDtypeStruct(r.shape, r.dtype) for r in results],
+        in_specs=[hbm] * 4,
+        out_specs=[hbm] * 4,
+        scratch_shapes=[pltpu.VMEM(r.shape, r.dtype) for r in results] + [dma((4,)), dma((4,))],
+    )(*results)
+    return attended, hidden, mig_lat, mig_rope.T
 
 
 def solution(mesh):

time: 41.2 us -> 34.5 us (0.84)
  local copies, waits for them, and re-layouts: 6.73 us -> 0 us
    unnamed x3 -> x0, local copies, waits for them, and re-layouts: 5.31 us -> none
    pallas_call x0 -> x1, Pallas kernels: none -> 2.3 us  [body(): pl.pallas_call(functools.partial(place_kernel, 4), out_shape=[jax.ShapeDt...]
    pallas_call x1, Pallas kernels: 32.9 us -> 30.8 us  [body(): pl.pallas_call(functools.partial(kernel, p), out_shape=(jax.ShapeDtypeStr...]
    pallas_call x1 -> x0, local copies, waits for them, and re-layouts: 1.42 us -> none  [body(): pl.pallas_call(functools.partial(kernel, p), out_shape=(jax.ShapeDtypeStr...]
where the time goes in v2:
time: 34.5 us; the launch traced here: 34.4 us
  Pallas kernels  33.1 us (96%)
  between operations  1.29 us (4%)
    pallas_call x1, Pallas kernels, body(): pl.pallas_call(functools.partial(kernel, p), out_shape=(jax.ShapeDtypeStr...  30.8 us
    pallas_call x1, Pallas kernels, body(): pl.pallas_call(functools.partial(place_kernel, 4), out_shape=[jax.ShapeDt...  2.3 us

profile of v2, /device:TPU:1, one launch (start us, length us, event | category | flops | bytes accessed | tf_op | source)
XLA Modules:
  0.0 34.4 jit_solution(8856310622604195701)
XLA Ops:
  1.3 30.8 %shard_map.147 = (bf16[64,8192]{1,0:T(8,128)(2,1)}, bf16[1,144,256]{2,1,0:T(8,128)(2,1)}, bf16[80,512]{1,0:T(8,128)(2,1)}, bf16[64,80]{1,0:T(8,128)(2,1)}) custom-call(s32[1]{0:T(128)S(6)} %copy.16.limit_ref, s32[4]{0:T(128)} %owners_ref.1, s32[2,64]{1,0:T(2,128)} %bitcast.2, bf16[64,1792]{1,0:T(8,128)(2,1)} %feat_ref.1, bf16[16,512]{1,0:T(8,128)(2,1)} %prelat_ref.1, ...), custom_call_target="tpu_custom_call" | custom-call | tf_op jit(solution)/shard_map/pallas_call | solution.py:478
  32.1 2.3 %shard_map.148 = (bf16[64,8192]{1,0:T(8,128)(2,1)}, bf16[1,144,256]{2,1,0:T(8,128)(2,1)}, bf16[80,512]{1,0:T(8,128)(2,1)}, bf16[64,80]{1,0:T(8,128)(2,1)}) custom-call(bf16[64,8192]{1,0:T(8,128)(2,1)} %get-tuple-element.12.refs_0_, bf16[1,144,256]{2,1,0:T(8,128)(2,1)} %get-tuple-element.13.refs_1_, bf16[80,512]{1,0:T(8,128)(2,1)} %get-tuple-element.14.refs_2_, ...), custom_call_target="tpu_custom_call" | custom-call | tf_op jit(solution)/shard_map/pallas_call | solution.py:508

commit v3 on v2

--- a/solution.py
+++ b/solution.py
@@ -277,7 +277,8 @@
                 kv_c(other, j, k).wait_send()
         each_from(1, n, one)
 
-    units = [(k, i) for k in range(1, n) for i in range(p.halves)]
+    order = list(range(1, n, 2)) + list(range(2, n, 2))
+    units = [(k, i) for k in order for i in range(p.halves)]
     ahead = AHEAD if n <= 4 else len(units)
     if KV_AT == 0:
         by_head(kv_first)

time: 34.5 us -> 32.7 us (0.948)
  Pallas kernels: 33.1 us -> 31 us
    pallas_call x1, Pallas kernels: 30.8 us -> 28.7 us  [body(): pl.pallas_call(functools.partial(kernel, p), out_shape=(jax.ShapeDtypeStr...]
where the time goes in v3:
time: 32.7 us; the launch traced here: 32.3 us
  Pallas kernels  31 us (95%)
  between operations  1.29 us (4%)
    pallas_call x1, Pallas kernels, body(): pl.pallas_call(functools.partial(kernel, p), out_shape=(jax.ShapeDtypeStr...  28.7 us
    pallas_call x1, Pallas kernels, body(): pl.pallas_call(functools.partial(place_kernel, 4), out_shape=[jax.ShapeDt...  2.3 us

profile of v3, /device:TPU:1, one launch (start us, length us, event | category | flops | bytes accessed | tf_op | source)
XLA Modules:
  0.0 32.3 jit_solution(16785252246895778067)
XLA Ops:
  1.3 28.7 %shard_map.147 = (bf16[64,8192]{1,0:T(8,128)(2,1)}, bf16[1,144,256]{2,1,0:T(8,128)(2,1)}, bf16[80,512]{1,0:T(8,128)(2,1)}, bf16[64,80]{1,0:T(8,128)(2,1)}) custom-call(s32[1]{0:T(128)S(6)} %copy.16.limit_ref, s32[4]{0:T(128)} %owners_ref.1, s32[2,64]{1,0:T(2,128)} %bitcast.2, bf16[64,1792]{1,0:T(8,128)(2,1)} %feat_ref.1, bf16[16,512]{1,0:T(8,128)(2,1)} %prelat_ref.1, ...), custom_call_target="tpu_custom_call" | custom-call | tf_op jit(solution)/shard_map/pallas_call | solution.py:479
  30.0 2.3 %shard_map.148 = (bf16[64,8192]{1,0:T(8,128)(2,1)}, bf16[1,144,256]{2,1,0:T(8,128)(2,1)}, bf16[80,512]{1,0:T(8,128)(2,1)}, bf16[64,80]{1,0:T(8,128)(2,1)}) custom-call(bf16[64,8192]{1,0:T(8,128)(2,1)} %get-tuple-element.12.refs_0_, bf16[1,144,256]{2,1,0:T(8,128)(2,1)} %get-tuple-element.13.refs_1_, bf16[80,512]{1,0:T(8,128)(2,1)} %get-tuple-element.14.refs_2_, ...), custom_call_target="tpu_custom_call" | custom-call | tf_op jit(solution)/shard_map/pallas_call | solution.py:509
